TPU v7x, 32 devices: a whole 2x2x4 slice. The times are simulated.
32 devices in a mesh: grp: 2 (over y), row: 8 (over z, x), col: 2 (over core).
Axes of the slice: x: 2, y: 2, z: 4, core: 2. Of those that a mesh axis runs over, the one named last changes fastest.
Arguments:
- tokens: bfloat16 [128, 256, 180], P(('grp', 'row'), 'col'), parts along dimension 0, may hold values from -6 to 6
- grad_out: bfloat16 [128, 256, 180], P(('grp', 'row'), 'col'), parts along dimension 0, may hold values from -8 to 8
- regions: int32 [128, 256], P(('grp', 'row'), 'col'), parts along dimension 0, may hold values from 0 to 15, as said below
- ln_gain: float32 [180], replicated, may hold values from 0.1 to 1.9
- ln_offset: float32 [180], replicated, may hold values from -1.5 to 1.5
- qkv_weight: bfloat16 [180, 540], replicated, may hold values from -0.4375 to 0.4375
- qkv_bias: float32 [540], replicated, may hold values from -1.5 to 1.5
- proj_weight: bfloat16 [180, 180], replicated, may hold values from -0.4375 to 0.4375
- bias_table: float32 [225, 6], replicated, may hold values from -4 to 320
Outputs:
- d_tokens: bfloat16 [128, 256, 180], P(('grp', 'row'), 'col'), parts along dimension 0
- d_qkv_weight: float32 [360, 540], P('grp'), parts along dimension 0
- d_qkv_bias: float32 [1080], P('grp'), parts along dimension 0
- d_proj_weight: float32 [360, 180], P('grp'), parts along dimension 0
- d_bias_table: float32 [450, 6], P('grp'), parts along dimension 0
- d_ln_gain: float32 [360], P('grp'), parts along dimension 0
- d_ln_offset: float32 [360], P('grp'), parts along dimension 0
There are 2 independent parts, one for each index of `grp`. A program takes and returns all parts, laid end to end along the dimension named above; an argument that names none is the same for every part. Nothing has to cross between parts.
Inputs may be any that keep to these rules, and one draw needn't show every extreme that they name: `regions`: A token attends only to tokens of its window with the same id. The map is a grid: the id is 4 a + b, where a, from 0 to 3, depends only on the token's row and b, from 0 to 3, only on its column.
All inputs are finite; a program needn't handle non-finite values.
Results may differ from a plain program's by a relative error of at most 0.0085.
Values may be sent and summed in bfloat16 or wider, within the bound.
A program may use at most 64 MiB of HBM per device.

v0:
```python
import jax
import jax.numpy as jnp
from jax import lax
from jax.sharding import PartitionSpec as P

HEADS = 6
WIN = 8
SHIFT = 4
masked_score = -10000.0


def from_behind(shard, axis, by):
    count = lax.axis_size(axis)
    return lax.ppermute(shard, axis, [(i, (i + by) % count) for i in range(count)])


def multiply(form, left, right):
    return jnp.einsum(form, left, right, preferred_element_type=jnp.float32)


def relative_onehot(table_rows):
    span_size = WIN * WIN
    position = jnp.arange(span_size, dtype=jnp.int32)
    row_pos = position // WIN
    col_pos = position % WIN
    entry_index = (
        (row_pos[:, None] - row_pos[None, :] + WIN - 1) * (2 * WIN - 1)
        + col_pos[:, None]
        - col_pos[None, :]
        + WIN
        - 1
    )
    return (
        entry_index.reshape(-1)[:, None] == jnp.arange(table_rows, dtype=jnp.int32)[None, :]
    ).astype(jnp.float32)


def normalize(values, gain_vec, offset_vec):
    as_float = values.astype(jnp.float32)
    center = jnp.mean(as_float, -1, keepdims=True)
    variance = jnp.mean(jnp.square(as_float - center), -1, keepdims=True)
    inv_std = lax.rsqrt(variance + 1e-05)
    unit_tokens = (as_float - center) * inv_std
    normed = (unit_tokens * gain_vec + offset_vec).astype(jnp.bfloat16)
    return (normed, unit_tokens, inv_std)


def project(normed, weights, offsets):
    channels = normed.shape[-1]
    summed = multiply("rcd,df->rcf", normed, weights) + offsets
    factor = jnp.where(jnp.arange(3 * channels) < channels, (channels // HEADS) ** (-0.5), 1.0)
    return (summed * factor).astype(jnp.bfloat16)


def window_band(qkv, grad_band, label_band, rel_bias, proj_weight):
    channels = grad_band.shape[-1]
    head_count = rel_bias.shape[0]
    head_size = channels // head_count
    tile_cols = grad_band.shape[1]
    win_count = tile_cols // WIN
    span_size = WIN * WIN

    def windows(array):
        array = array.reshape((WIN, win_count, WIN) + array.shape[2:])
        array = jnp.moveaxis(array, 1, 0)
        return array.reshape((win_count, span_size) + array.shape[3:])

    parted = windows(qkv).reshape(win_count, span_size, 3, head_count, head_size)
    query_part = parted[:, :, 0]
    key_part = parted[:, :, 1]
    value_part = parted[:, :, 2]
    grad_win = windows(grad_band)
    label_win = windows(label_band)
    matched = label_win[:, :, None] == label_win[:, None, :]
    scores = multiply("nihd,njhd->nhij", query_part, key_part) + rel_bias[None]
    scores = jnp.where(matched[:, None], scores, masked_score)
    probability = jax.nn.softmax(scores, axis=-1)
    prob_low = probability.astype(jnp.bfloat16)
    attended = (
        multiply("nhij,njhd->nihd", prob_low, value_part)
        .astype(jnp.bfloat16)
        .reshape(win_count * span_size, channels)
    )
    flat_grad = grad_win.reshape(win_count * span_size, channels)
    d_proj = multiply("tc,td->cd", attended, flat_grad)
    d_attended = (
        multiply("td,cd->tc", flat_grad, proj_weight)
        .astype(jnp.bfloat16)
        .reshape(win_count, span_size, head_count, head_size)
    )
    d_prob = multiply("nihd,njhd->nhij", d_attended, value_part)
    d_scores = probability * (d_prob - jnp.sum(probability * d_prob, -1, keepdims=True))
    score_sum = jnp.sum(d_scores, 0)
    d_score_low = d_scores.astype(jnp.bfloat16)
    d_query = multiply("nhij,njhd->nihd", d_score_low, key_part) * head_size ** (-0.5)
    d_key = multiply("nhij,nihd->njhd", d_score_low, query_part)
    d_value = multiply("nhij,nihd->njhd", prob_low, d_attended)
    d_qkv = (
        jnp.stack([d_query, d_key, d_value], 2)
        .astype(jnp.bfloat16)
        .reshape(win_count, span_size, 3 * channels)
    )
    array = d_qkv
    array = array.reshape((win_count, WIN, WIN) + array.shape[2:])
    array = jnp.moveaxis(array, 0, 1)
    return (array.reshape((WIN, tile_cols) + array.shape[3:]), d_proj, score_sum)


def attention_backward(qkv, grad_tile, label_tile, rel_bias, proj_weight):
    tile_rows = grad_tile.shape[0]
    band_count = tile_rows // WIN
    channels = grad_tile.shape[-1]
    head_count = rel_bias.shape[0]

    def to_bands(array):
        return array.reshape((band_count, WIN) + array.shape[1:])

    def band_step(running, pieces):
        d_qkv, d_proj, score_sum = window_band(
            pieces[0], pieces[1], pieces[2], rel_bias, proj_weight
        )
        return ((running[0] + d_proj, running[1] + score_sum), d_qkv)

    initial = (
        jnp.zeros((channels, channels), jnp.float32),
        jnp.zeros((head_count, WIN * WIN, WIN * WIN), jnp.float32),
    )
    totals, d_qkv = lax.scan(
        band_step, initial, (to_bands(qkv), to_bands(grad_tile), to_bands(label_tile))
    )
    return (d_qkv.reshape((tile_rows,) + d_qkv.shape[2:]), totals[0], totals[1])


def input_backward(d_qkv, normed, unit_tokens, inv_std, gain_vec, qkv_weight):
    d_weight = multiply("rcd,rcf->df", normed, d_qkv)
    d_offsets = jnp.sum(d_qkv.astype(jnp.float32), (0, 1))
    d_normed = multiply("rcf,df->rcd", d_qkv, qkv_weight)
    d_gain = jnp.sum(d_normed * unit_tokens, (0, 1))
    d_offset = jnp.sum(d_normed, (0, 1))
    scaled_grad = d_normed * gain_vec
    d_input = inv_std * (
        scaled_grad
        - jnp.mean(scaled_grad, -1, keepdims=True)
        - unit_tokens * jnp.mean(scaled_grad * unit_tokens, -1, keepdims=True)
    )
    return (d_input, d_weight, d_offsets, d_gain, d_offset)


def into_frame(member_one, member_two, member_three):
    below_one, below_two, below_three = from_behind(
        (member_one[:SHIFT], member_two[:SHIFT], member_three[:SHIFT]), "row", -1
    )
    member_one = jnp.concatenate([member_one[SHIFT:], below_one], 0)
    member_two = jnp.concatenate([member_two[SHIFT:], below_two], 0)
    member_three = jnp.concatenate([member_three[SHIFT:], below_three], 0)
    right_one, right_two, right_three = from_behind(
        (member_one[:, :SHIFT], member_two[:, :SHIFT], member_three[:, :SHIFT]), "col", -1
    )
    member_one = jnp.concatenate([member_one[:, SHIFT:], right_one], 1)
    member_two = jnp.concatenate([member_two[:, SHIFT:], right_two], 1)
    member_three = jnp.concatenate([member_three[:, SHIFT:], right_three], 1)
    return (member_one, member_two, member_three)


def back_proj(field):
    from_left = from_behind(field[:, -SHIFT:], "col", 1)
    field = jnp.concatenate([from_left, field[:, :-SHIFT]], 1)
    from_above = from_behind(field[-SHIFT:], "row", 1)
    return jnp.concatenate([from_above, field[:-SHIFT]], 0)


def table_grad(score_sum, entry_table):
    head_count = score_sum.shape[0]
    flat_sum = jnp.transpose(score_sum, (1, 2, 0)).reshape(-1, head_count)
    return jnp.dot(entry_table.T, flat_sum, precision=lax.Precision.HIGHEST)


def attention_sums(d_proj, d_table):
    return (d_proj, d_table)


def on_device(
    tokens, grad_out, regions, ln_gain, ln_offset, qkv_weight, qkv_bias, proj_weight, bias_table
):
    head_count = bias_table.shape[1]
    entry_table = relative_onehot(bias_table.shape[0])
    rel_bias = (
        jnp.dot(entry_table, bias_table, precision=lax.Precision.HIGHEST)
        .reshape(WIN * WIN, WIN * WIN, head_count)
        .transpose(2, 0, 1)
    )
    labels = regions.astype(jnp.bfloat16)
    normed, unit_tokens, inv_std = normalize(tokens, ln_gain, ln_offset)
    qkv = project(normed, qkv_weight, qkv_bias)
    qkv_framed, grad_framed, label_framed = into_frame(qkv, grad_out, labels)
    d_framed, d_proj, score_sum = attention_backward(
        qkv_framed, grad_framed, label_framed, rel_bias, proj_weight
    )
    d_proj, d_table = attention_sums(d_proj, table_grad(score_sum, entry_table))
    d_qkv = back_proj(d_framed)
    d_input, d_weight, d_offsets, d_gain, d_offset = input_backward(
        d_qkv, normed, unit_tokens, inv_std, ln_gain, qkv_weight
    )
    d_proj, d_table, d_weight, d_offsets, d_gain, d_offset = lax.psum(
        (d_proj, d_table, d_weight, d_offsets, d_gain, d_offset), ("row", "col")
    )
    total_tokens = tokens.shape[0] * tokens.shape[1] * lax.axis_size("row") * lax.axis_size("col")
    out_scale = total_tokens ** (-0.5)
    d_tokens = (grad_out.astype(jnp.float32) + d_input).astype(jnp.bfloat16)
    return (
        d_tokens,
        d_weight * out_scale,
        d_offsets * out_scale,
        d_proj * out_scale,
        d_table * out_scale,
        d_gain * out_scale,
        d_offset * out_scale,
    )


def solution(mesh):
    placed = (
        P(("grp", "row"), "col", None),
        P(("grp", "row"), "col", None),
        P(("grp", "row"), "col"),
        P(),
        P(),
        P(),
        P(),
        P(),
        P(),
    )
    return jax.shard_map(
        on_device,
        mesh=mesh,
        in_specs=placed,
        out_specs=(
            P(("grp", "row"), "col", None),
            P("grp", None),
            P("grp"),
            P("grp", None),
            P("grp", None),
            P("grp"),
            P("grp"),
        ),
        check_vma=False,
    )
```

profile of v0, /device:TPU:0, one launch (start us, length us, event | category | flops | bytes accessed | tf_op | source)
XLA Modules:
  0.0 272.9 jit_solution(3321277854407880220)
XLA Ops:
  7.2 1.1 convert_reduce_fusion.1
  8.3 1.1 fusion.40
  9.5 0.6 copy-done.15
  10.1 1.6 multiply_convert_fusion
  12.1 6.0 %collective-permute-start = (bf16[4,128,540]{1,0,2:T(4,128)(2,1)S(1)}, bf16[4,128,540]{1,0,2:T(4,128)(2,1)S(1)}, u32[]{:S(2)}, u32[]{:S(2)}) collective-permute-start(bf16[4,128,540]{1,0,2:T(4,128)(2,1)S(1)} %copy.87), channel_id=1, source_target_pairs={{0,14},{2,0},{4,2},{6,4},{8,6},{10,8},{12,10},{14,12},{1,15},{3,1}... | collective-permute-start | bytes 1658888 | tf_op jit(solution)/shard_map/ppermute | solution.py:14
  18.2 0.6 collective-permute-start.2
  19.1 1.4 collective-permute-start.4
  20.7 0.6 copy-done.17
  21.3 2.6 fusion.2
  24.3 6.8 %collective-permute-done.2 = bf16[4,128]{1,0:T(4,128)(2,1)S(1)} collective-permute-done((bf16[4,128]{1,0:T(4,128)(2,1)S(1)}, bf16[4,128]{1,0:T(4,128)(2,1)S(1)}, u32[]{:S(2)}, u32[]{:S(2)}) %collective-permute-start.2) | collective-permute-done | bytes 1056 | tf_op jit(solution)/shard_map/ppermute | solution.py:14
  31.2 1.1 collective-permute-done.3
  32.9 2.7 %collective-permute-done.4 = bf16[4,128,180]{2,1,0:T(8,128)(2,1)S(1)} collective-permute-done((bf16[4,128,180]{2,1,0:T(8,128)(2,1)S(1)}, bf16[4,128,180]{2,1,0:T(8,128)(2,1)S(1)}, u32[]{:S(2)}, u32[]{:S(2)}) %collective-permute-start.4) | collective-permute-done | bytes 184352 | tf_op jit(solution)/shard_map/ppermute | solution.py:14
  35.8 1.0 collective-permute-done.5
  37.0 0.8 copy-done.2
  37.8 0.3 convolution_convert_fusion.3
  38.2 1.3 reshape.196
  39.7 0.5 copy.89
  40.4 0.4 slice_maximum_fusion
  40.7 0.7 collective-permute-done.1
  41.4 0.6 copy.90
  42.0 1.6 pad_maximum_fusion.3
  43.6 1.7 copy.91
  45.4 5.6 %reshape.191 = bf16[16,64,3,6,30]{4,3,2,1,0:T(8,128)(2,1)} reshape(bf16[16,8,8,540]{3,2,1,0:T(8,128)(2,1)S(1)} %copy.92) | data formatting | bytes 2211840 | tf_op jit(solution)/shard_map/while/body/eval_jaxpr/reshape;while/body/eval_jaxpr/reshape | solution.py:68
  51.1 6.6 %fusion.52 = (bf16[16,64,1,6,30]{4,3,2,1,0:T(8,128)(2,1)S(1)}, bf16[16,64,1,6,30]{4,3,2,1,0:T(8,128)(2,1)}, bf16[16,64,1,6,30]{4,3,2,1,0:T(8,128)(2,1)}) fusion(bf16[16,64,3,6,30]{4,3,2,1,0:T(8,128)(2,1)} %reshape.191), kind=kLoop, calls=%fused_computation.97 | loop fusion | bytes 2211840 | tf_op jit(solution)/shard_map/while/body/eval_jaxpr/slice | solution.py:71
  57.6 2.4 copy.123
  60.0 3.1 %copy.124 = bf16[16,64,1,6,30]{1,4,3,0,2:T(8,128)(2,1)} copy(bf16[16,64,1,6,30]{4,3,2,1,0:T(8,128)(2,1)} %get-tuple-element.77) | data formatting | bytes 737280
  63.2 1.9 copy.127
  65.1 1.7 fusion.26
  66.8 1.1 fusion.56
  68.2 1.0 multiply_reduce_fusion
  69.2 1.1 fusion.13
  70.3 0.5 fusion.12
  70.8 0.6 copy-done.1
  71.4 0.9 fusion.9
  72.4 0.9 fusion.10
  73.3 0.6 pad_maximum_fusion
  73.9 5.5 %copy.108 = bf16[16,64,3,6,30]{4,3,2,1,0:T(8,128)(2,1)} copy(bf16[16,64,3,6,30]{1,4,3,0,2:T(8,128)(2,1)S(1)} %pad_maximum_fusion) | data formatting | bytes 2211840 | tf_op jit(solution)/shard_map/while/body/eval_jaxpr/stack | solution.py:99
  79.4 7.9 %convert_element_type.55 = bf16[16,8,8,540]{3,2,1,0:T(8,128)(2,1)} reshape(bf16[16,64,3,6,30]{4,3,2,1,0:T(8,128)(2,1)} %copy.108) | data formatting | bytes 2211840 | tf_op jit(solution)/shard_map/while/body/eval_jaxpr/convert_element_type | solution.py:100
  87.3 1.4 copy_bitcast_fusion
  89.0 0.8 copy.128
  90.1 0.6 copy.112
  91.0 1.1 copy.113
  92.1 0.3 collective-permute-start.7
  92.4 0.4 copy-done.6
  92.8 1.5 fusion.11
  94.5 2.5 copy.116
  97.0 1.8 reshape.198
  98.8 1.4 fusion.1
  100.2 1.0 fusion.57
  101.2 9.2 %collective-permute-done.7 = bf16[4,128,540]{1,0,2:T(4,128)(2,1)} collective-permute-done((bf16[4,128,540]{1,0,2:T(4,128)(2,1)}, bf16[4,128,540]{1,0,2:T(4,128)(2,1)}, u32[]{:S(2)}, u32[]{:S(2)}) %collective-permute-start.7) | collective-permute-done | bytes 552992 | tf_op jit(solution)/shard_map/ppermute | solution.py:14
  110.4 1.1 copy.114
  111.6 0.6 convert_reduce_fusion
  112.2 0.4 copy-done.4
  112.6 0.7 fusion.39
  113.3 1.4 convolution_bitcast_fusion
  114.7 58.2 %all-reduce = (f32[540]{0:T(1024)S(1)}, f32[225,6]{0,1:T(8,128)S(1)}, f32[180]{0:T(256)S(1)}, f32[180]{0:T(256)S(1)}) all-reduce(f32[540]{0:T(1024)S(1)} %get-tuple-element.72, f32[225,6]{0,1:T(8,128)S(1)} %fusion.1, f32[180]{0:T(256)S(1)} %get-tuple-element.62, ...), channel_id=1, replica_groups=mesh['grp'=2,'row'=8,'col'=2] {'row','col'}, use_global_device_ids=true, to_apply=%region_9.10 | all-reduce | flops 2250 | bytes 18000 | tf_op jit(solution)/shard_map/psum | solution.py:204
  172.9 0.6 broadcast_multiply_fusion.3
  173.4 0.6 broadcast_multiply_fusion.7
  174.3 0.6 broadcast_multiply_fusion.8
  174.9 0.8 copy.118
  175.7 0.6 broadcast_multiply_fusion.2
  176.3 86.3 %all-reduce.4.cloned.1.call-done = (f32[180,540]{1,0:T(8,128)}, f32[180,180]{1,0:T(8,128)}) async-done(((f32[180,540]{1,0:T(8,128)}, f32[180,180]{1,0:T(8,128)}), (f32[180,540]{1,0:T(8,128)}, f32[180,180]{1,0:T(8,128)})) %all-reduce.4.cloned.1.call-update) | async-done | bytes 518416 | tf_op jit(solution)/shard_map/psum | solution.py:204
  262.6 1.8 broadcast_multiply_fusion
  264.5 1.6 broadcast_multiply_fusion.1
  (85 shorter events, 4.5 us)
Async XLA Ops:
  7.2 2.9 %copy-start = (bf16[180,540]{1,0:T(8,128)(2,1)S(1)}, bf16[180,540]{1,0:T(8,128)(2,1)}, u32[]{:S(2)}) copy-start(bf16[180,540]{1,0:T(8,128)(2,1)} %param.14) | copy-start | bytes 583204
  7.2 255.5 %all-reduce.4.cloned.1.call-start = ((), (), s32[]{:S(2)}) async-start(), calls=%async_computation | async-start | bytes 1318912 | tf_op jit(solution)/shard_map/psum | solution.py:204
  8.3 1.1 copy-start.13
  9.5 0.6 copy-start.15
  11.7 6.4 %copy-start.19 = (s32[8,128]{1,0:T(8,128)S(1)}, s32[8,128]{1,0:T(8,128)}, u32[]{:S(2)}) copy-start(s32[8,128]{1,0:T(8,128)} %param.11) | copy-start | bytes 12292
  11.7 7.0 %copy-start.7 = (bf16[8,128,180]{1,0,2:T(8,128)(2,1)S(1)}, bf16[8,128,180]{1,0,2:T(8,128)(2,1)}, u32[]{:S(2)}) copy-start(bf16[8,128,180]{1,0,2:T(8,128)(2,1)} %param.10) | copy-start | bytes 1105924
  11.7 9.5 %copy-start.21 = (f32[225,6]{0,1:T(8,128)S(1)}, f32[225,6]{0,1:T(8,128)}, u32[]{:S(2)}) copy-start(f32[225,6]{0,1:T(8,128)} %param.17) | copy-start | bytes 16204
  12.1 27.4 %collective-permute-start = (bf16[4,128,540]{1,0,2:T(4,128)(2,1)S(1)}, bf16[4,128,540]{1,0,2:T(4,128)(2,1)S(1)}, u32[]{:S(2)}, u32[]{:S(2)}) collective-permute-start(bf16[4,128,540]{1,0,2:T(4,128)(2,1)S(1)} %copy.87), channel_id=1, source_target_pairs={{0,14},{2,0},{4,2},{6,4},{8,6},{10,8},{12,10},{14,12},{1,15},{3,1}... | collective-permute-start | bytes 1658888 | tf_op jit(solution)/shard_map/ppermute | solution.py:14
  18.2 12.9 %collective-permute-start.2 = (bf16[4,128]{1,0:T(4,128)(2,1)S(1)}, bf16[4,128]{1,0:T(4,128)(2,1)S(1)}, u32[]{:S(2)}, u32[]{:S(2)}) collective-permute-start(bf16[4,128]{1,0:T(4,128)(2,1)S(1)} %get-tuple-element.84), channel_id=1, source_target_pairs={{0,14},{2,0},{4,2},{6,4},{8,6},{10,8},{12,10},{14,12},{1,15},{3,1}... | collective-permute-start | bytes 3080 | tf_op jit(solution)/shard_map/ppermute | solution.py:14
  19.1 16.5 %collective-permute-start.4 = (bf16[4,128,180]{2,1,0:T(8,128)(2,1)S(1)}, bf16[4,128,180]{2,1,0:T(8,128)(2,1)S(1)}, u32[]{:S(2)}, u32[]{:S(2)}) collective-permute-start(bf16[4,128,180]{2,1,0:T(8,128)(2,1)S(1)} %copy.126), channel_id=1, source_target_pairs={{0,14},{2,0},{4,2},{6,4},{8,6},{10,8},{12,10},{14,12},{1,15},{3,1}... | collective-permute-start | bytes 552968 | tf_op jit(solution)/shard_map/ppermute | solution.py:14
  20.7 0.6 copy-start.17
  24.1 13.8 %copy-start.12 = (bf16[180,180]{1,0:T(8,128)(2,1)S(1)}, bf16[180,180]{1,0:T(8,128)(2,1)}, u32[]{:S(2)}) copy-start(bf16[180,180]{1,0:T(8,128)(2,1)} %param.16) | copy-start | bytes 194404
  31.1 1.2 collective-permute-start.3
  35.6 1.2 collective-permute-start.5
  37.0 0.8 copy-start.2
  40.1 1.3 collective-permute-start.1
  66.8 1.1 copy-start.9
  66.8 1.3 copy-start.11
  67.9 4.4 %copy-start.5 = (f32[16,6,64,64]{2,3,1,0:T(8,128)}, f32[16,6,64,64]{2,3,1,0:T(8,128)S(1)}, u32[]{:S(2)}) copy-start(f32[16,6,64,64]{2,3,1,0:T(8,128)S(1)} %get-tuple-element.86) | copy-start | bytes 4718596
  70.3 1.1 copy-start.1
  88.8 1.3 collective-permute-start.6
  90.1 2.3 copy-start.10
  90.6 2.2 copy-start.6
  92.1 18.4 %collective-permute-start.7 = (bf16[4,128,540]{1,0,2:T(4,128)(2,1)}, bf16[4,128,540]{1,0,2:T(4,128)(2,1)}, u32[]{:S(2)}, u32[]{:S(2)}) collective-permute-start(bf16[4,128,540]{1,0,2:T(4,128)(2,1)} %copy.113), channel_id=1, source_target_pairs={{0,2},{2,4},{4,6},{6,8},{8,10},{10,12},{12,14},{14,0},{1,3},{3,5},... | collective-permute-start | bytes 1658888 | tf_op jit(solution)/shard_map/ppermute | solution.py:14
  94.3 4.5 %copy-start.18 = (s32[4096]{0:T(1024)S(1)}, s32[4096]{0:T(1024)}, u32[]{:S(2)}) copy-start(s32[4096]{0:T(1024)} %copy-done.17) | copy-start | bytes 49156
  94.4 5.8 %copy-start.3 = (bf16[16,8,8,180]{3,2,1,0:T(8,128)(2,1)S(1)}, bf16[16,8,8,180]{3,2,1,0:T(8,128)(2,1)}, u32[]{:S(2)}) copy-start(bf16[16,8,8,180]{3,2,1,0:T(8,128)(2,1)} %copy-done.2) | copy-start | bytes 1105924
  111.6 1.0 copy-start.4
  111.6 1.0 copy-start.14
  111.6 1.0 copy-start.16
  111.6 1.0 copy-start.20
  112.2 1.1 copy-start.22
  113.3 60.8 %copy-start.8 = (bf16[8,128,180]{1,0,2:T(8,128)(2,1)S(1)}, bf16[8,128,180]{1,0,2:T(8,128)(2,1)}, u32[]{:S(2)}) copy-start(bf16[8,128,180]{1,0,2:T(8,128)(2,1)} %param.10) | copy-start | bytes 1105924
Sparse Core Ops, SparseCore 0:
  174.2 88.4 all-reduce.3
where the time goes:
time: 274 us; the launch traced here: 273 us
  waiting for transfers between devices  108 us (39%)
  blocking collectives  58.2 us (21%)
  local copies, waits for them, and re-layouts  52.8 us (19%)
  matrix products  15.6 us (6%)
  other arithmetic  14.7 us (5%)
  between operations  14.5 us (5%)
  starting transfers between devices  8.96 us (3%)
    psum x1, waiting for transfers between devices, on_device(): lax.psum((d_proj, d_table, d_weight, d_offsets, d_gain, d_offset), ('row'...  86.3 us
    psum x1, blocking collectives, on_device(): lax.psum((d_proj, d_table, d_weight, d_offsets, d_gain, d_offset), ('row'...  58.2 us
    ppermute x8, waiting for transfers between devices, from_behind(): lax.ppermute(shard, axis, [(i, (i + by) % count) for i in range(count)])  21.8 us
    unnamed x53, local copies, waits for them, and re-layouts  13.1 us
    dot_general x11, matrix products, multiply(): return jnp.einsum(form, left, right, preferred_element_type=jnp.float32)  11.6 us
    ppermute x8, starting transfers between devices, from_behind(): lax.ppermute(shard, axis, [(i, (i + by) % count) for i in range(count)])  8.92 us
    convert_element_type x1, local copies, waits for them, and re-layouts, window_band(): d_qkv = jnp.stack([d_query, d_key, d_value], 2).astype(jnp.bfloat16).resh...  7.91 us
    slice x1, local copies, waits for them, and re-layouts, window_band(): value_part = parted[:, :, 2]  6.55 us
  transfers between devices with their start and end apart: 9, of which 8 were waited for; matrix products, arithmetic and copies ran while one was open for 7% of the time, Pallas kernels for 0%

commit v1 on v0

--- a/solution.py
+++ b/solution.py
@@ -2,6 +2,7 @@
 import jax.numpy as jnp
 from jax import lax
 from jax.sharding import PartitionSpec as P
+from jax.lax import psum
 
 HEADS = 6
 WIN = 8
@@ -201,8 +202,8 @@
     d_input, d_weight, d_offsets, d_gain, d_offset = input_backward(
         d_qkv, normed, unit_tokens, inv_std, ln_gain, qkv_weight
     )
-    d_proj, d_table, d_weight, d_offsets, d_gain, d_offset = lax.psum(
-        (d_proj, d_table, d_weight, d_offsets, d_gain, d_offset), ("row", "col")
+    d_proj, d_table, d_weight, d_offsets, d_gain, d_offset = psum(
+        psum((d_proj, d_table, d_weight, d_offsets, d_gain, d_offset), "col"), "row"
     )
     total_tokens = tokens.shape[0] * tokens.shape[1] * lax.axis_size("row") * lax.axis_size("col")
     out_scale = total_tokens ** (-0.5)

time: 274 us -> 236 us (0.86)
  blocking collectives: 58.2 us -> 37.9 us
  waiting for transfers between devices: 108 us -> 90.2 us
    psum x1 -> x2, blocking collectives: 58.2 us -> 37.9 us  [the longest x1 34.6 us: on_device(): psum(psum((d_proj, d_table, d_weight, d_offsets, d_gain, d_offset), 'col'...]
    psum x1 -> x2, waiting for transfers between devices: 86.3 us -> 68.4 us  [the longest x1 68.4 us: on_device(): psum(psum((d_proj, d_table, d_weight, d_offsets, d_gain, d_offset), 'col'...]
  transfers between devices with their start and end apart: 9 -> 10, of which waited for: 8 -> 8; matrix products, arithmetic and copies ran while one was open for 7% -> 8% of each run, Pallas kernels for 0% -> 0%
where the time goes in v1:
time: 236 us; the launch traced here: 235 us
  waiting for transfers between devices  90.2 us (38%)
  local copies, waits for them, and re-layouts  52.8 us (22%)
  blocking collectives  37.9 us (16%)
  matrix products  15.6 us (7%)
  other arithmetic  14.7 us (6%)
  between operations  14.5 us (6%)
  starting transfers between devices  9 us (4%)
    psum x1, waiting for transfers between devices, on_device(): psum(psum((d_proj, d_table, d_weight, d_offsets, d_gain, d_offset), 'col'...  68.4 us
    psum x1, blocking collectives, on_device(): psum(psum((d_proj, d_table, d_weight, d_offsets, d_gain, d_offset), 'col'...  34.6 us
    ppermute x8, waiting for transfers between devices, from_behind(): lax.ppermute(shard, axis, [(i, (i + by) % count) for i in range(count)])  21.8 us
    unnamed x53, local copies, waits for them, and re-layouts  13.1 us
    dot_general x11, matrix products, multiply(): return jnp.einsum(form, left, right, preferred_element_type=jnp.float32)  11.6 us
    ppermute x8, starting transfers between devices, from_behind(): lax.ppermute(shard, axis, [(i, (i + by) % count) for i in range(count)])  8.92 us
    convert_element_type x1, local copies, waits for them, and re-layouts, window_band(): d_qkv = jnp.stack([d_query, d_key, d_value], 2).astype(jnp.bfloat16).resh...  7.91 us
    slice x1, local copies, waits for them, and re-layouts, window_band(): value_part = parted[:, :, 2]  6.55 us
  transfers between devices with their start and end apart: 10, of which 8 were waited for; matrix products, arithmetic and copies ran while one was open for 8% of the time, Pallas kernels for 0%

profile of v1, /device:TPU:0, one launch (start us, length us, event | category | flops | bytes accessed | tf_op | source)
XLA Modules:
  0.0 234.7 jit_solution(12905361585052562238)
XLA Ops:
  7.2 1.1 convert_reduce_fusion.1
  8.3 1.1 fusion.40
  9.5 0.6 copy-done.15
  10.1 1.6 multiply_convert_fusion
  12.1 6.0 %collective-permute-start = (bf16[4,128,540]{1,0,2:T(4,128)(2,1)S(1)}, bf16[4,128,540]{1,0,2:T(4,128)(2,1)S(1)}, u32[]{:S(2)}, u32[]{:S(2)}) collective-permute-start(bf16[4,128,540]{1,0,2:T(4,128)(2,1)S(1)} %copy.87), channel_id=1, source_target_pairs={{0,14},{2,0},{4,2},{6,4},{8,6},{10,8},{12,10},{14,12},{1,15},{3,1}... | collective-permute-start | bytes 1658888 | tf_op jit(solution)/shard_map/ppermute | solution.py:15
  18.2 0.6 collective-permute-start.2
  19.1 1.4 collective-permute-start.4
  20.7 0.6 copy-done.17
  21.3 2.6 %fusion.2 = f32[4096,6]{0,1:T(8,128)S(1)} fusion(f32[225,6]{0,1:T(8,128)S(1)} %copy-done.21, s32[4096]{0:T(1024)S(1)} %reshape.202), kind=kOutput, calls=%fused_computation.3 | convolution fusion | flops 67276800 | bytes 120088 | tf_op jit(solution)/shard_map/dot_general | solution.py:189
  24.3 6.8 %collective-permute-done.2 = bf16[4,128]{1,0:T(4,128)(2,1)S(1)} collective-permute-done((bf16[4,128]{1,0:T(4,128)(2,1)S(1)}, bf16[4,128]{1,0:T(4,128)(2,1)S(1)}, u32[]{:S(2)}, u32[]{:S(2)}) %collective-permute-start.2) | collective-permute-done | bytes 1056 | tf_op jit(solution)/shard_map/ppermute | solution.py:15
  31.2 1.1 collective-permute-done.3
  32.9 2.7 %collective-permute-done.4 = bf16[4,128,180]{2,1,0:T(8,128)(2,1)S(1)} collective-permute-done((bf16[4,128,180]{2,1,0:T(8,128)(2,1)S(1)}, bf16[4,128,180]{2,1,0:T(8,128)(2,1)S(1)}, u32[]{:S(2)}, u32[]{:S(2)}) %collective-permute-start.4) | collective-permute-done | bytes 184352 | tf_op jit(solution)/shard_map/ppermute | solution.py:15
  35.8 1.0 collective-permute-done.5
  37.0 0.8 copy-done.2
  38.2 1.3 reshape.196
  39.7 0.5 copy.89
  40.4 0.4 slice_maximum_fusion
  40.7 0.7 collective-permute-done.1
  41.4 0.6 copy.90
  42.0 1.6 pad_maximum_fusion.3
  43.6 1.7 copy.91
  45.4 5.6 %reshape.191 = bf16[16,64,3,6,30]{4,3,2,1,0:T(8,128)(2,1)} reshape(bf16[16,8,8,540]{3,2,1,0:T(8,128)(2,1)S(1)} %copy.92) | data formatting | bytes 2211840 | tf_op jit(solution)/shard_map/while/body/eval_jaxpr/reshape;while/body/eval_jaxpr/reshape | solution.py:69
  51.1 6.6 %fusion.52 = (bf16[16,64,1,6,30]{4,3,2,1,0:T(8,128)(2,1)S(1)}, bf16[16,64,1,6,30]{4,3,2,1,0:T(8,128)(2,1)}, bf16[16,64,1,6,30]{4,3,2,1,0:T(8,128)(2,1)}) fusion(bf16[16,64,3,6,30]{4,3,2,1,0:T(8,128)(2,1)} %reshape.191), kind=kLoop, calls=%fused_computation.97 | loop fusion | bytes 2211840 | tf_op jit(solution)/shard_map/while/body/eval_jaxpr/slice | solution.py:72
  57.6 2.4 %copy.123 = bf16[16,64,1,6,30]{1,4,3,0,2:T(8,128)(2,1)S(1)} copy(bf16[16,64,1,6,30]{4,3,2,1,0:T(8,128)(2,1)} %get-tuple-element.84) | data formatting | bytes 737280
  60.0 3.1 %copy.124 = bf16[16,64,1,6,30]{1,4,3,0,2:T(8,128)(2,1)} copy(bf16[16,64,1,6,30]{4,3,2,1,0:T(8,128)(2,1)} %get-tuple-element.83) | data formatting | bytes 737280
  63.2 1.9 copy.127
  65.1 1.7 fusion.26
  66.8 1.1 fusion.56
  68.2 1.0 multiply_reduce_fusion
  69.2 1.1 fusion.13
  70.3 0.5 fusion.12
  70.8 0.6 copy-done.1
  71.4 0.9 fusion.9
  72.4 0.9 fusion.10
  73.3 0.6 pad_maximum_fusion
  73.9 5.5 %copy.108 = bf16[16,64,3,6,30]{4,3,2,1,0:T(8,128)(2,1)} copy(bf16[16,64,3,6,30]{1,4,3,0,2:T(8,128)(2,1)S(1)} %pad_maximum_fusion) | data formatting | bytes 2211840 | tf_op jit(solution)/shard_map/while/body/eval_jaxpr/stack | solution.py:100
  79.4 7.9 %convert_element_type.55 = bf16[16,8,8,540]{3,2,1,0:T(8,128)(2,1)} reshape(bf16[16,64,3,6,30]{4,3,2,1,0:T(8,128)(2,1)} %copy.108) | data formatting | bytes 2211840 | tf_op jit(solution)/shard_map/while/body/eval_jaxpr/convert_element_type | solution.py:101
  87.3 1.4 copy_bitcast_fusion
  89.0 0.8 copy.128
  90.1 0.6 copy.112
  91.0 1.1 copy.113
  92.1 0.3 collective-permute-start.7
  92.4 0.4 copy-done.6
  92.8 1.5 fusion.11
  94.5 2.5 %copy.116 = bf16[16,64,6,30]{1,0,3,2:T(8,128)(2,1)} copy(bf16[16,64,6,30]{1,3,2,0:T(8,128)(2,1)} %fusion.11) | data formatting | bytes 737280 | tf_op jit(solution)/shard_map/while/body/eval_jaxpr/convert_element_type | solution.py:82
  97.0 1.8 reshape.198
  98.8 1.4 fusion.1
  100.2 1.0 fusion.57
  101.2 9.2 %collective-permute-done.7 = bf16[4,128,540]{1,0,2:T(4,128)(2,1)} collective-permute-done((bf16[4,128,540]{1,0,2:T(4,128)(2,1)}, bf16[4,128,540]{1,0,2:T(4,128)(2,1)}, u32[]{:S(2)}, u32[]{:S(2)}) %collective-permute-start.7) | collective-permute-done | bytes 552992 | tf_op jit(solution)/shard_map/ppermute | solution.py:15
  110.4 1.1 copy.114
  111.6 0.6 convert_reduce_fusion
  112.2 0.4 copy-done.4
  112.6 0.7 fusion.39
  113.3 1.4 convolution_bitcast_fusion
  114.8 3.3 %all-reduce.2 = (f32[540]{0:T(1024)S(1)}, f32[225,6]{0,1:T(8,128)S(1)}, f32[180]{0:T(256)S(1)}, f32[180]{0:T(256)S(1)}) all-reduce(f32[540]{0:T(1024)S(1)} %get-tuple-element.78, f32[225,6]{0,1:T(8,128)S(1)} %fusion.1, f32[180]{0:T(256)S(1)} %get-tuple-element.62, ...), channel_id=1, replica_groups=mesh['grp'=2,'row'=8,'col'=2] {'col'}, use_global_device_ids=true, to_apply=%region_10.11 | all-reduce | flops 2250 | bytes 18000 | tf_op jit(solution)/shard_map/psum | solution.py:206
  118.1 34.6 %all-reduce = (f32[540]{0:T(1024)S(1)}, f32[225,6]{0,1:T(8,128)S(1)}, f32[180]{0:T(256)S(1)}, f32[180]{0:T(256)S(1)}) all-reduce(f32[540]{0:T(1024)S(1)} %get-tuple-element.72, f32[225,6]{0,1:T(8,128)S(1)} %get-tuple-element.73, f32[180]{0:T(256)S(1)} %get-tuple-element.74, ...), channel_id=1, replica_groups=mesh['grp'=2,'row'=8,'col'=2] {'row'}, use_global_device_ids=true, to_apply=%region_11.12 | all-reduce | flops 2250 | bytes 18000 | tf_op jit(solution)/shard_map/psum | solution.py:205
  152.6 0.6 broadcast_multiply_fusion.7
  153.5 0.6 broadcast_multiply_fusion.8
  154.1 0.8 copy.118
  154.9 0.6 broadcast_multiply_fusion.3
  155.5 0.6 broadcast_multiply_fusion.2
  156.1 68.4 %all-reduce.7.cloned.1.call-done = (f32[180,540]{1,0:T(8,128)}, f32[180,180]{1,0:T(8,128)}) async-done(((f32[180,540]{1,0:T(8,128)}, f32[180,180]{1,0:T(8,128)}), (f32[180,540]{1,0:T(8,128)}, f32[180,180]{1,0:T(8,128)})) %all-reduce.7.cloned.1.call-update) | async-done | bytes 518416 | tf_op jit(solution)/shard_map/psum | solution.py:205
  224.5 1.8 broadcast_multiply_fusion
  226.3 1.6 broadcast_multiply_fusion.1
  (89 shorter events, 4.9 us)
Async XLA Ops:
  7.2 2.9 %copy-start = (bf16[180,540]{1,0:T(8,128)(2,1)S(1)}, bf16[180,540]{1,0:T(8,128)(2,1)}, u32[]{:S(2)}) copy-start(bf16[180,540]{1,0:T(8,128)(2,1)} %param.14) | copy-start | bytes 583204
  7.2 146.3 %all-reduce.9.cloned.1.call-start = ((), (), s32[]{:S(2)}) async-start(), calls=%async_computation.1 | async-start | bytes 1318912 | tf_op jit(solution)/shard_map/psum | solution.py:206
  8.3 1.1 copy-start.13
  9.5 0.6 copy-start.15
  11.7 6.4 %copy-start.19 = (s32[8,128]{1,0:T(8,128)S(1)}, s32[8,128]{1,0:T(8,128)}, u32[]{:S(2)}) copy-start(s32[8,128]{1,0:T(8,128)} %param.11) | copy-start | bytes 12292
  11.7 7.0 %copy-start.7 = (bf16[8,128,180]{1,0,2:T(8,128)(2,1)S(1)}, bf16[8,128,180]{1,0,2:T(8,128)(2,1)}, u32[]{:S(2)}) copy-start(bf16[8,128,180]{1,0,2:T(8,128)(2,1)} %param.10) | copy-start | bytes 1105924
  11.7 9.5 %copy-start.21 = (f32[225,6]{0,1:T(8,128)S(1)}, f32[225,6]{0,1:T(8,128)}, u32[]{:S(2)}) copy-start(f32[225,6]{0,1:T(8,128)} %param.17) | copy-start | bytes 16204
  12.1 27.4 %collective-permute-start = (bf16[4,128,540]{1,0,2:T(4,128)(2,1)S(1)}, bf16[4,128,540]{1,0,2:T(4,128)(2,1)S(1)}, u32[]{:S(2)}, u32[]{:S(2)}) collective-permute-start(bf16[4,128,540]{1,0,2:T(4,128)(2,1)S(1)} %copy.87), channel_id=1, source_target_pairs={{0,14},{2,0},{4,2},{6,4},{8,6},{10,8},{12,10},{14,12},{1,15},{3,1}... | collective-permute-start | bytes 1658888 | tf_op jit(solution)/shard_map/ppermute | solution.py:15
  18.2 12.9 %collective-permute-start.2 = (bf16[4,128]{1,0:T(4,128)(2,1)S(1)}, bf16[4,128]{1,0:T(4,128)(2,1)S(1)}, u32[]{:S(2)}, u32[]{:S(2)}) collective-permute-start(bf16[4,128]{1,0:T(4,128)(2,1)S(1)} %get-tuple-element.90), channel_id=1, source_target_pairs={{0,14},{2,0},{4,2},{6,4},{8,6},{10,8},{12,10},{14,12},{1,15},{3,1}... | collective-permute-start | bytes 3080 | tf_op jit(solution)/shard_map/ppermute | solution.py:15
  19.1 16.5 %collective-permute-start.4 = (bf16[4,128,180]{2,1,0:T(8,128)(2,1)S(1)}, bf16[4,128,180]{2,1,0:T(8,128)(2,1)S(1)}, u32[]{:S(2)}, u32[]{:S(2)}) collective-permute-start(bf16[4,128,180]{2,1,0:T(8,128)(2,1)S(1)} %copy.126), channel_id=1, source_target_pairs={{0,14},{2,0},{4,2},{6,4},{8,6},{10,8},{12,10},{14,12},{1,15},{3,1}... | collective-permute-start | bytes 552968 | tf_op jit(solution)/shard_map/ppermute | solution.py:15
  20.7 0.6 copy-start.17
  24.1 13.8 %copy-start.12 = (bf16[180,180]{1,0:T(8,128)(2,1)S(1)}, bf16[180,180]{1,0:T(8,128)(2,1)}, u32[]{:S(2)}) copy-start(bf16[180,180]{1,0:T(8,128)(2,1)} %param.16) | copy-start | bytes 194404
  31.1 1.2 collective-permute-start.3
  35.6 1.2 collective-permute-start.5
  37.0 0.8 copy-start.2
  40.1 1.3 collective-permute-start.1
  66.8 1.1 copy-start.9
  66.8 1.3 copy-start.11
  67.9 4.4 %copy-start.5 = (f32[16,6,64,64]{2,3,1,0:T(8,128)}, f32[16,6,64,64]{2,3,1,0:T(8,128)S(1)}, u32[]{:S(2)}) copy-start(f32[16,6,64,64]{2,3,1,0:T(8,128)S(1)} %get-tuple-element.92) | copy-start | bytes 4718596
  70.3 1.1 copy-start.1
  88.8 1.3 collective-permute-start.6
  90.1 2.3 copy-start.10
  90.6 2.2 copy-start.6
  92.1 18.4 %collective-permute-start.7 = (bf16[4,128,540]{1,0,2:T(4,128)(2,1)}, bf16[4,128,540]{1,0,2:T(4,128)(2,1)}, u32[]{:S(2)}, u32[]{:S(2)}) collective-permute-start(bf16[4,128,540]{1,0,2:T(4,128)(2,1)} %copy.113), channel_id=1, source_target_pairs={{0,2},{2,4},{4,6},{6,8},{8,10},{10,12},{12,14},{14,0},{1,3},{3,5},... | collective-permute-start | bytes 1658888 | tf_op jit(solution)/shard_map/ppermute | solution.py:15
  94.3 4.5 %copy-start.18 = (s32[4096]{0:T(1024)S(1)}, s32[4096]{0:T(1024)}, u32[]{:S(2)}) copy-start(s32[4096]{0:T(1024)} %copy-done.17) | copy-start | bytes 49156
  94.4 5.8 %copy-start.3 = (bf16[16,8,8,180]{3,2,1,0:T(8,128)(2,1)S(1)}, bf16[16,8,8,180]{3,2,1,0:T(8,128)(2,1)}, u32[]{:S(2)}) copy-start(bf16[16,8,8,180]{3,2,1,0:T(8,128)(2,1)} %copy-done.2) | copy-start | bytes 1105924
  111.6 1.0 copy-start.4
  111.6 1.0 copy-start.14
  111.6 1.0 copy-start.16
  111.6 1.0 copy-start.20
  112.2 1.1 copy-start.22
  113.3 39.9 %copy-start.8 = (bf16[8,128,180]{1,0,2:T(8,128)(2,1)S(1)}, bf16[8,128,180]{1,0,2:T(8,128)(2,1)}, u32[]{:S(2)}) copy-start(bf16[8,128,180]{1,0,2:T(8,128)(2,1)} %param.10) | copy-start | bytes 1105924
  114.7 109.7 %all-reduce.7.cloned.1.call-start = ((), (), s32[]{:S(2)}) async-start(), calls=%async_computation | async-start | bytes 1318912 | tf_op jit(solution)/shard_map/psum | solution.py:205
Sparse Core Ops, SparseCore 0:
  114.8 17.4 all-reduce.8
  153.7 70.7 all-reduce.6
